TPU v7x, 128 devices: a whole 4x4x4 slice. The times are simulated.
128 devices in a mesh: fsdp: 8 (over y_lo, z), ctx: 16 (over y_hi, x, core).
Axes of the slice: x: 4, y: 4 (y_hi: 2, y_lo: 2; y = y_hi * 2 + y_lo), z: 4, core: 2. Of those that a mesh axis runs over, the one named last changes fastest.
Arguments:
- tokens: bfloat16 [16384, 1024], P(('fsdp', 'ctx')), may hold values from -6 to 6
- cotangent: bfloat16 [16384, 1024], P(('fsdp', 'ctx')), may hold values from -6 to 6
- w_query: bfloat16 [1024, 2048], P('fsdp'), may hold values from -0.1875 to 0.1875
- w_key: bfloat16 [1024, 1024], P('fsdp'), may hold values from -0.1875 to 0.1875
- w_value: bfloat16 [1024, 1024], P('fsdp'), may hold values from -0.1875 to 0.1875
- w_output: bfloat16 [1024, 2048], P('fsdp'), may hold values from -2 to 2
- w_gate: bfloat16 [1024, 3072], P('fsdp'), may hold values from -0.1875 to 0.1875
- w_up: bfloat16 [1024, 3072], P('fsdp'), may hold values from -0.1875 to 0.1875
- w_down: bfloat16 [1024, 3072], P('fsdp'), may hold values from -0.109375 to 0.109375
- norm_gain: float32 [1024], replicated, may hold values from 0.5 to 1.5
- mlp_gain: float32 [1024], replicated, may hold values from 0.5 to 1.5
- query_gain: float32 [128], replicated, may hold values from 0.1 to 1.9
- key_gain: float32 [128], replicated, may hold values from 0.1 to 1.9
Outputs:
- mixed: bfloat16 [16384, 1024], P(('fsdp', 'ctx'))
- input_grad: float32 [16384, 1024], P(('fsdp', 'ctx'))
- grad_query: float32 [1024, 2048], P('fsdp')
- grad_key: float32 [1024, 1024], P('fsdp')
- grad_value: float32 [1024, 1024], P('fsdp')
- grad_output: float32 [1024, 2048], P('fsdp')
- grad_gate: float32 [1024, 3072], P('fsdp')
- grad_up: float32 [1024, 3072], P('fsdp')
- grad_down: float32 [1024, 3072], P('fsdp')
- grad_norm_gain: float32 [1024], replicated
- grad_mlp_gain: float32 [1024], replicated
- grad_query_gain: float32 [128], replicated
- grad_key_gain: float32 [128], replicated
All inputs are finite; a program needn't handle non-finite values.
Results may differ from a plain program's by a relative error of at most 0.028.
Values may be sent and summed in bfloat16 or wider, within the bound.
A program may use at most 192 MiB of HBM per device.

v0:
```python
import math

import jax
import jax.numpy as jnp
from jax import lax
from jax.sharding import PartitionSpec as P

EPSILON = 1e-06
THETA = 1000000.0
NEGATIVE = -1e30


def rms_scale(rows):
    return lax.rsqrt(jnp.mean(rows * rows, -1, keepdims=True) + EPSILON)


def rope_tables(positions, head_dim):
    half = head_dim // 2
    freqs = jnp.power(THETA, -2.0 * jnp.arange(half, dtype=jnp.float32) / head_dim)
    angles = positions.astype(jnp.float32)[:, None] * freqs[None, :]
    return (jnp.cos(angles), jnp.sin(angles))


def rotate(heads, cosine, sine):
    half = heads.shape[-1] // 2
    first = heads[..., :half]
    second = heads[..., half:]
    cosine = cosine[:, None, :]
    sine = sine[:, None, :]
    return jnp.concatenate(
        [first * cosine - second * sine, second * cosine + first * sine], axis=-1
    )


def rotate_back(grads, cosine, sine):
    half = grads.shape[-1] // 2
    first = grads[..., :half]
    second = grads[..., half:]
    cosine = cosine[:, None, :]
    sine = sine[:, None, :]
    return jnp.concatenate(
        [first * cosine + second * sine, second * cosine - first * sine], axis=-1
    )


def head_norm(raw_heads, gain):
    scaling = rms_scale(raw_heads)
    normed = raw_heads * scaling
    return (normed, scaling, normed * gain)


def head_norm_back(grads, normed, scaling, gain):
    d_normed = grads * gain
    gain_grad = jnp.sum(grads * normed, axis=(0, 1))
    raw_grad = scaling * (d_normed - normed * jnp.mean(d_normed * normed, -1, keepdims=True))
    return (raw_grad, gain_grad)


def contract_last(left, right):
    return lax.dot_general(
        left, right, (((1,), (1,)), ((), ())), preferred_element_type=jnp.float32
    )


def on_device(
    tokens,
    cotangent,
    w_query,
    w_key,
    w_value,
    w_output,
    w_gate,
    w_up,
    w_down,
    norm_gain,
    mlp_gain,
    query_gain,
    key_gain,
):
    tok_rows = tokens.shape[0]
    head_dim = query_gain.shape[0]
    q_heads = w_query.shape[1] // head_dim
    kv_heads = w_key.shape[1] // head_dim
    group = q_heads // kv_heads
    seq_len = tok_rows * lax.axis_size("ctx")
    first_pos = lax.axis_index("ctx") * tok_rows
    positions = first_pos + jnp.arange(tok_rows, dtype=jnp.int32)
    last_pos = first_pos + tok_rows - 1
    cosine, sine = rope_tables(positions, head_dim)
    scale_factor = 1.0 / math.sqrt(head_dim)
    inputs = tokens.astype(jnp.float32)
    scale_one = rms_scale(inputs)
    normed_one = inputs * scale_one
    normed_in = (normed_one * norm_gain).astype(jnp.bfloat16)
    full_query, full_key, full_value, full_output = (
        lax.all_gather(w_query, "fsdp", axis=0, tiled=True),
        lax.all_gather(w_key, "fsdp", axis=0, tiled=True),
        lax.all_gather(w_value, "fsdp", axis=0, tiled=True),
        lax.all_gather(w_output, "fsdp", axis=0, tiled=True),
    )
    query_raw = jnp.dot(normed_in, full_query, preferred_element_type=jnp.float32).reshape(
        tok_rows, q_heads, head_dim
    )
    key_raw = jnp.dot(normed_in, full_key, preferred_element_type=jnp.float32).reshape(
        tok_rows, kv_heads, head_dim
    )
    value_heads = (
        jnp.dot(normed_in, full_value, preferred_element_type=jnp.float32)
        .astype(jnp.bfloat16)
        .reshape(tok_rows, kv_heads, head_dim)
    )
    query_normed, query_scale, query_scaled = head_norm(query_raw, query_gain)
    key_normed, key_scale, key_scaled = head_norm(key_raw, key_gain)
    query_heads = rotate(query_scaled, cosine, sine).astype(jnp.bfloat16)
    key_heads = rotate(key_scaled, cosine, sine).astype(jnp.bfloat16)
    query_four = query_heads.reshape(tok_rows, kv_heads, group, head_dim)

    def split_piece(piece):
        key_rows, value_rows = piece
        length = key_rows.shape[0]
        block_len = math.gcd(length, 512)
        count = length // block_len
        starts = block_len * jnp.arange(count, dtype=jnp.int32)
        return (
            key_rows.reshape(count, block_len, kv_heads, head_dim),
            value_rows.reshape(count, block_len, kv_heads, head_dim),
            starts,
        )

    def block_scores(key_rows, key_start):
        block_len = key_rows.shape[0]
        scores = (
            jnp.einsum("qhgd,khd->hgqk", query_four, key_rows, preferred_element_type=jnp.float32)
            * scale_factor
        )
        key_pos = key_start + jnp.arange(block_len, dtype=jnp.int32)
        allowed = key_pos[None, :] <= positions[:, None]
        return (jnp.where(allowed, scores, NEGATIVE), allowed)

    start_state = (
        jnp.full((kv_heads, group, tok_rows), NEGATIVE, jnp.float32),
        jnp.zeros((kv_heads, group, tok_rows), jnp.float32),
        jnp.zeros((kv_heads, group, tok_rows, head_dim), jnp.float32),
    )
    carry = start_state

    def attend_step(state, element):
        key_rows, value_rows, key_start = element

        def attend_update(current):
            best, total, accum = current
            scores, allowed = block_scores(key_rows, key_start)
            new_best = jnp.maximum(best, jnp.max(scores, -1))
            raised = jnp.where(allowed, jnp.exp(scores - new_best[..., None]), 0.0)
            decay = jnp.exp(best - new_best)
            total = total * decay + jnp.sum(raised, -1)
            accum = accum * decay[..., None] + jnp.einsum(
                "hgqk,khd->hgqd",
                raised.astype(jnp.bfloat16),
                value_rows,
                preferred_element_type=jnp.float32,
            )
            return (new_best, total, accum)

        return (
            lax.cond(key_start <= last_pos, attend_update, lambda current: current, state),
            None,
        )

    carry, _ = lax.scan(
        attend_step,
        carry,
        split_piece(
            (
                lax.all_gather(key_heads, "ctx", axis=0, tiled=True),
                lax.all_gather(value_heads, "ctx", axis=0, tiled=True),
            )
        ),
    )
    best, total, accum = carry
    attn_exact = accum / total[..., None]
    log_total = best + jnp.log(total)
    attended = (
        attn_exact.transpose(2, 0, 1, 3).reshape(tok_rows, q_heads * head_dim).astype(jnp.bfloat16)
    )
    branch = contract_last(attended, full_output)
    resid = inputs + branch
    full_gate, full_up, full_down = (
        lax.all_gather(w_gate, "fsdp", axis=0, tiled=True),
        lax.all_gather(w_up, "fsdp", axis=0, tiled=True),
        lax.all_gather(w_down, "fsdp", axis=0, tiled=True),
    )
    scale_two = rms_scale(resid)
    normed_two = resid * scale_two
    mlp_in = (normed_two * mlp_gain).astype(jnp.bfloat16)
    gate = jnp.dot(mlp_in, full_gate, preferred_element_type=jnp.float32)
    up_proj = jnp.dot(mlp_in, full_up, preferred_element_type=jnp.float32)
    sigmoid_gate = jax.nn.sigmoid(gate)
    activated = gate * sigmoid_gate
    hidden = (activated * up_proj).astype(jnp.bfloat16)
    mlp_out = contract_last(hidden, full_down)
    mixed = (resid + mlp_out).astype(jnp.bfloat16)
    cot_rows = cotangent.astype(jnp.float32)
    d_hidden = jnp.dot(cotangent, full_down, preferred_element_type=jnp.float32)
    d_gate = (d_hidden * up_proj * sigmoid_gate * (1.0 + gate * (1.0 - sigmoid_gate))).astype(
        jnp.bfloat16
    )
    d_up = (d_hidden * activated).astype(jnp.bfloat16)
    d_mlp_in = contract_last(d_gate, full_gate) + contract_last(d_up, full_up)
    mlp_gain_part = jnp.sum(d_mlp_in * normed_two, 0)
    d_normed_two = d_mlp_in * mlp_gain
    d_resid = (
        scale_two
        * (d_normed_two - normed_two * jnp.mean(d_normed_two * normed_two, -1, keepdims=True))
        + cot_rows
    )
    d_branch = d_resid.astype(jnp.bfloat16)
    d_attended = jnp.dot(d_branch, full_output, preferred_element_type=jnp.float32).astype(
        jnp.bfloat16
    )
    d_four = d_attended.reshape(tok_rows, kv_heads, group, head_dim)
    delta = jnp.sum(d_four.astype(jnp.float32).transpose(1, 2, 0, 3) * attn_exact, -1)
    grad_start = (
        jnp.zeros((kv_heads, group, tok_rows, head_dim), jnp.float32),
        jnp.zeros((seq_len, kv_heads, head_dim), jnp.float32),
        jnp.zeros((seq_len, kv_heads, head_dim), jnp.float32),
    )
    carry = grad_start

    def gradient_step(state, element):
        key_rows, value_rows, key_start = element
        block_len = key_rows.shape[0]

        def gradient_update(current):
            d_query, key_acc, value_acc = current
            scores, allowed = block_scores(key_rows, key_start)
            soft = jnp.where(allowed, jnp.exp(scores - log_total[..., None]), 0.0)
            d_soft = jnp.einsum(
                "qhgd,khd->hgqk", d_four, value_rows, preferred_element_type=jnp.float32
            )
            d_scores = (soft * (d_soft - delta[..., None])).astype(jnp.bfloat16)
            d_query = d_query + scale_factor * jnp.einsum(
                "hgqk,khd->hgqd", d_scores, key_rows, preferred_element_type=jnp.float32
            )
            key_part = scale_factor * jnp.einsum(
                "hgqk,qhgd->khd", d_scores, query_four, preferred_element_type=jnp.float32
            )
            value_part = jnp.einsum(
                "hgqk,qhgd->khd",
                soft.astype(jnp.bfloat16),
                d_four,
                preferred_element_type=jnp.float32,
            )
            key_acc = lax.dynamic_update_slice_in_dim(
                key_acc,
                lax.dynamic_slice_in_dim(key_acc, key_start, block_len, 0) + key_part,
                key_start,
                0,
            )
            value_acc = lax.dynamic_update_slice_in_dim(
                value_acc,
                lax.dynamic_slice_in_dim(value_acc, key_start, block_len, 0) + value_part,
                key_start,
                0,
            )
            return (d_query, key_acc, value_acc)

        return (
            lax.cond(key_start <= last_pos, gradient_update, lambda current: current, state),
            None,
        )

    carry, _ = lax.scan(
        gradient_step,
        carry,
        split_piece(
            (
                lax.all_gather(key_heads, "ctx", axis=0, tiled=True),
                lax.all_gather(value_heads, "ctx", axis=0, tiled=True),
            )
        ),
    )
    d_query, key_acc, value_acc = carry
    d_key, d_value = (
        lax.psum_scatter(
            key_acc.astype(jnp.bfloat16), "ctx", scatter_dimension=0, tiled=True
        ).astype(jnp.float32),
        lax.psum_scatter(
            value_acc.astype(jnp.bfloat16), "ctx", scatter_dimension=0, tiled=True
        ).astype(jnp.float32),
    )
    d_query_rot = d_query.transpose(2, 0, 1, 3).reshape(tok_rows, q_heads, head_dim)
    d_query_raw, query_gain_part = head_norm_back(
        rotate_back(d_query_rot, cosine, sine), query_normed, query_scale, query_gain
    )
    d_key_raw, key_gain_part = head_norm_back(
        rotate_back(d_key, cosine, sine), key_normed, key_scale, key_gain
    )
    d_query_b = d_query_raw.reshape(tok_rows, q_heads * head_dim).astype(jnp.bfloat16)
    d_key_b = d_key_raw.reshape(tok_rows, kv_heads * head_dim).astype(jnp.bfloat16)
    d_value_b = d_value.reshape(tok_rows, kv_heads * head_dim).astype(jnp.bfloat16)
    d_normed_in = (
        contract_last(d_query_b, full_query)
        + contract_last(d_key_b, full_key)
        + contract_last(d_value_b, full_value)
    )
    norm_gain_part = jnp.sum(d_normed_in * normed_one, 0)
    d_normed_one = d_normed_in * norm_gain
    input_grad = (
        scale_one
        * (d_normed_one - normed_one * jnp.mean(d_normed_one * normed_one, -1, keepdims=True))
        + d_resid
    )
    gain_grads = lax.psum(
        (norm_gain_part, mlp_gain_part, query_gain_part, key_gain_part), ("fsdp", "ctx")
    )

    def rows_of(left, right):
        return lax.dot_general(
            left, right, (((0,), (0,)), ((), ())), preferred_element_type=jnp.float32
        )

    shard_rows = lax.psum_scatter(
        jnp.concatenate(
            [
                rows_of(normed_in, d_query_b),
                rows_of(normed_in, d_key_b),
                rows_of(normed_in, d_value_b),
                rows_of(d_branch, attended),
                rows_of(mlp_in, d_gate),
                rows_of(mlp_in, d_up),
                rows_of(cotangent, hidden),
            ],
            axis=1,
        ).astype(jnp.bfloat16),
        "fsdp",
        scatter_dimension=0,
        tiled=True,
    ).astype(jnp.float32)
    shard_rows = lax.psum(shard_rows.astype(jnp.bfloat16), "ctx").astype(jnp.float32)
    sizes_cols = [
        q_heads * head_dim,
        kv_heads * head_dim,
        kv_heads * head_dim,
        q_heads * head_dim,
        gate.shape[1],
        gate.shape[1],
        gate.shape[1],
    ]
    pieces_out = []
    offset = 0
    for columns in sizes_cols:
        pieces_out.append(shard_rows[:, offset : offset + columns])
        offset = offset + columns
    return (
        mixed,
        input_grad,
        pieces_out[0],
        pieces_out[1],
        pieces_out[2],
        pieces_out[3],
        pieces_out[4],
        pieces_out[5],
        pieces_out[6],
        gain_grads[0],
        gain_grads[1],
        gain_grads[2],
        gain_grads[3],
    )


def solution(mesh):
    in_specs = (
        P(("fsdp", "ctx"), None),
        P(("fsdp", "ctx"), None),
        P("fsdp", None),
        P("fsdp", None),
        P("fsdp", None),
        P("fsdp", None),
        P("fsdp", None),
        P("fsdp", None),
        P("fsdp", None),
        P(),
        P(),
        P(),
        P(),
    )
    out_specs = (
        P(("fsdp", "ctx"), None),
        P(("fsdp", "ctx"), None),
        P("fsdp", None),
        P("fsdp", None),
        P("fsdp", None),
        P("fsdp", None),
        P("fsdp", None),
        P("fsdp", None),
        P("fsdp", None),
        P(),
        P(),
        P(),
        P(),
    )
    return jax.shard_map(
        on_device, mesh=mesh, in_specs=in_specs, out_specs=out_specs, check_vma=False
    )
```

profile of v0, /device:TPU:1, one launch (start us, length us, event | category | flops | bytes accessed | tf_op | source)
XLA Modules:
  0.0 1411.1 jit_solution(13170084086440031662)
XLA Ops:
  10.9 38.4 %all-gather.10.cloned.1.call-done = bf16[1024,1024]{1,0:T(8,128)(2,1)} async-done(((bf16[128,1024]{1,0:T(8,128)(2,1)}), bf16[1024,1024]{1,0:T(8,128)(2,1)}) %all-gather.10.cloned.1.call-update) | async-done | bytes 2097168 | tf_op jit(solution)/shard_map/all_gather | solution.py:97
  53.3 38.5 %all-gather.16.cloned.1.call-done = bf16[1024,1024]{1,0:T(8,128)(2,1)} async-done(((bf16[128,1024]{1,0:T(8,128)(2,1)}), bf16[1024,1024]{1,0:T(8,128)(2,1)}) %all-gather.16.cloned.1.call-update) | async-done | bytes 2097168 | tf_op jit(solution)/shard_map/all_gather | solution.py:98
  97.6 53.2 %all-gather.14.cloned.1.call-done = bf16[1024,2048]{1,0:T(8,128)(2,1)} async-done(((bf16[128,2048]{1,0:T(8,128)(2,1)}), bf16[1024,2048]{1,0:T(8,128)(2,1)}) %all-gather.14.cloned.1.call-update) | async-done | bytes 4194320 | tf_op jit(solution)/shard_map/all_gather | solution.py:96
  156.5 52.2 %all-gather.12.cloned.1.call-done = bf16[2048,8,128]{2,0,1:T(8,128)(2,1)} async-done(((bf16[128,8,128]{2,0,1:T(8,128)(2,1)}), bf16[2048,8,128]{2,0,1:T(8,128)(2,1)}) %all-gather.12.cloned.1.call-update) | async-done | bytes 4194320 | tf_op jit(solution)/shard_map/all_gather | solution.py:175
  213.4 53.1 %all-gather.18.cloned.1.call-done = bf16[2048,8,128]{2,1,0:T(8,128)(2,1)} async-done(((bf16[128,8,128]{2,1,0:T(8,128)(2,1)}), bf16[2048,8,128]{2,1,0:T(8,128)(2,1)}) %all-gather.18.cloned.1.call-update) | async-done | bytes 4194320 | tf_op jit(solution)/shard_map/all_gather | solution.py:176
  271.8 12.2 while.30
  273.0 6.8 conditional.6
  286.7 32.5 %all-gather.20.cloned.1.call-done = bf16[1024,2048]{1,0:T(8,128)(2,1)} async-done(((bf16[128,2048]{1,0:T(8,128)(2,1)}), bf16[1024,2048]{1,0:T(8,128)(2,1)}) %all-gather.20.cloned.1.call-update) | async-done | bytes 4194320 | tf_op jit(solution)/shard_map/all_gather | solution.py:99
  323.1 68.8 %all-gather.22.cloned.1.call-done = bf16[1024,3072]{1,0:T(8,128)(2,1)} async-done(((bf16[128,3072]{1,0:T(8,128)(2,1)}), bf16[1024,3072]{1,0:T(8,128)(2,1)}) %all-gather.22.cloned.1.call-update) | async-done | bytes 6291472 | tf_op jit(solution)/shard_map/all_gather | solution.py:189
  396.9 67.9 %all-gather.24.cloned.1.call-done = bf16[1024,3072]{1,0:T(8,128)(2,1)} async-done(((bf16[128,3072]{1,0:T(8,128)(2,1)}), bf16[1024,3072]{1,0:T(8,128)(2,1)}) %all-gather.24.cloned.1.call-update) | async-done | bytes 6291472 | tf_op jit(solution)/shard_map/all_gather | solution.py:190
  469.7 67.8 %all-gather.26.cloned.1.call-done = bf16[1024,3072]{1,0:T(8,128)(2,1)} async-done(((bf16[128,3072]{1,0:T(8,128)(2,1)}), bf16[1024,3072]{1,0:T(8,128)(2,1)}) %all-gather.26.cloned.1.call-update) | async-done | bytes 6291472 | tf_op jit(solution)/shard_map/all_gather | solution.py:191
  537.6 6.4 multiply_convert_fusion
  566.4 49.0 %while.31 = (s32[]{:T(128)}, f32[8,2,128,128]{3,2,1,0:T(8,128)S(1)}, f32[2048,8,128]{2,0,1:T(8,128)}, f32[2048,8,128]{2,0,1:T(8,128)}, s32[4]{0:T(128)S(1)}, /*i...) while((s32[]{:T(128)}, ...), condition=%wide.region_15.16_spmd.clone, body=%wide.region_12.15_spmd.clone.sunk | while | flops 1356923520 | bytes 80969784 | solution.py:273
  568.2 43.3 %conditional.7 = ((f32[8,2,128,128]{3,2,1,0:T(8,128)S(1)}, f32[2048,8,128]{2,0,1:T(8,128)}, f32[2048,8,128]{2,0,1:T(8,128)})) conditional(s32[]{:T(128)} %convert_element_type.192, (f32[8,2,128,128]{3,2,1,0:T(8,128)S(1)}, f32[2048,8,128]{2,0,1:T(8,128)}, f32[2048,8,128]{2,0,1:T(8,128)}) %tuple.109, (s32[]{:T(128)}, s32[]{:T(128)}, ...), branch_computations={%region_13.13_spmd, %region_14.14_spmd} | conditional | flops 1356923520 | bytes 80968976 | solution.py:269
  583.7 11.2 dynamic_update_slice.8
  600.3 11.2 dynamic_update_slice.9
  615.4 6.0 convert_element_type.116
  621.5 7.4 copy.149
  628.9 6.4 copy.164
  644.0 183.5 %reduce-scatter.6.cloned.1.call-done = bf16[128,8,128]{2,0,1:T(8,128)(2,1)} async-done(((bf16[2048,8,128]{2,0,1:T(8,128)(2,1)}), bf16[128,8,128]{2,0,1:T(8,128)(2,1)}) %reduce-scatter.6.cloned.1.call-update) | async-done | bytes 262160 | tf_op jit(solution)/shard_map/reduce_scatter | solution.py:285
  833.7 77.6 %reduce-scatter.10.cloned.1.call-done = bf16[128,1024]{1,0:T(8,128)(2,1)} async-done(((bf16[2048,1024]{1,0:T(8,128)(2,1)}), bf16[128,1024]{1,0:T(8,128)(2,1)}) %reduce-scatter.10.cloned.1.call-update) | async-done | bytes 262160 | tf_op jit(solution)/shard_map/convert_element_type | solution.py:301
  937.6 309.9 %reduce-scatter.8.cloned.1.call-done = bf16[128,15360]{1,0:T(8,128)(2,1)} async-done(((bf16[1024,15360]{1,0:T(8,128)(2,1)}), bf16[128,15360]{1,0:T(8,128)(2,1)}) %reduce-scatter.8.cloned.1.call-update) | async-done | bytes 3932176 | tf_op jit(solution)/shard_map/reduce_scatter | solution.py:323
  1257.4 66.5 %all-reduce = (f32[1024]{0:T(1024)}, f32[1024]{0:T(1024)}, f32[128]{0:T(128)}, f32[128]{0:T(128)}) all-reduce(f32[1024]{0:T(1024)S(1)} %get-tuple-element.533, f32[1024]{0:T(1024)S(1)} %get-tuple-element.531, f32[128]{0:T(128)S(1)} %bitcast_reduce_fusion, ...), channel_id=1, replica_groups=mesh['fsdp'=8,'ctx'=16] {'fsdp','ctx'}, use_global_device_ids=true, to_apply=%region_24.25 | all-reduce | flops 2304 | bytes 18432 | tf_op jit(solution)/shard_map/psum | solution.py:314
  1324.9 73.1 %all-reduce.3.cloned.1.call-done = bf16[128,15360]{1,0:T(8,128)(2,1)} async-done(((bf16[128,15360]{1,0:T(8,128)(2,1)}), bf16[128,15360]{1,0:T(8,128)(2,1)}) %all-reduce.3.cloned.1.call-update) | async-done | bytes 3932176 | tf_op jit(solution)/shard_map/psum | solution.py:340
  (241 shorter events, 156.2 us)
Async XLA Ops:
  7.2 44.7 %copy-start.42 = (f32[128]{0:T(128)S(1)}, f32[128]{0:T(128)}, u32[]{:S(2)}) copy-start(f32[128]{0:T(128)} %param.33) | copy-start | bytes 1540
  7.2 42.1 %all-gather.10.cloned.1.call-start = ((), (), s32[]{:S(2)}) async-start(), calls=%async_computation.3 | async-start | bytes 2359296 | tf_op jit(solution)/shard_map/all_gather | solution.py:97
  7.9 83.9 %all-gather.16.cloned.1.call-start = ((), (), s32[]{:S(2)}) async-start(), calls=%async_computation.6 | async-start | bytes 2359296 | tf_op jit(solution)/shard_map/all_gather | solution.py:98
  8.7 142.1 %all-gather.14.cloned.1.call-start = ((), (), s32[]{:S(2)}) async-start(), calls=%async_computation.5 | async-start | bytes 4718592 | tf_op jit(solution)/shard_map/all_gather | solution.py:96
  9.4 199.3 %all-gather.12.cloned.1.call-start = ((), (), s32[]{:S(2)}) async-start(), calls=%async_computation.4 | async-start | bytes 4456448 | tf_op jit(solution)/shard_map/all_gather | solution.py:175
  10.9 81.0 %copy-start.6 = (bf16[128,1024]{1,0:T(8,128)(2,1)S(1)}, bf16[128,1024]{1,0:T(8,128)(2,1)}, u32[]{:S(2)}) copy-start(bf16[128,1024]{1,0:T(8,128)(2,1)} %param.21) | copy-start | bytes 786436
  10.9 80.9 %copy-start.39 = (f32[1024]{0:T(1024)S(1)}, f32[1024]{0:T(1024)}, u32[]{:S(2)}) copy-start(f32[1024]{0:T(1024)} %param.30) | copy-start | bytes 12292
  51.5 43.2 %copy-start.12 = (f32[128,1024]{1,0:T(8,128)}, f32[128,1024]{1,0:T(8,128)S(1)}, u32[]{:S(2)}) copy-start(f32[128,1024]{1,0:T(8,128)S(1)} %fusion.87) | copy-start | bytes 1572868
  53.3 213.2 %all-gather.18.cloned.1.call-start = ((), (), s32[]{:S(2)}) async-start(), calls=%async_computation.7 | async-start | bytes 4456448 | tf_op jit(solution)/shard_map/all_gather | solution.py:176
  94.7 224.5 %all-gather.20.cloned.1.call-start = ((), (), s32[]{:S(2)}) async-start(), calls=%async_computation.8 | async-start | bytes 4718592 | tf_op jit(solution)/shard_map/all_gather | solution.py:99
  95.3 296.7 %all-gather.22.cloned.1.call-start = ((), (), s32[]{:S(2)}) async-start(), calls=%async_computation.9 | async-start | bytes 7077888 | tf_op jit(solution)/shard_map/all_gather | solution.py:189
  96.1 368.7 %all-gather.24.cloned.1.call-start = ((), (), s32[]{:S(2)}) async-start(), calls=%async_computation.10 | async-start | bytes 7077888 | tf_op jit(solution)/shard_map/all_gather | solution.py:190
  96.8 440.8 %all-gather.26.cloned.1.call-start = ((), (), s32[]{:S(2)}) async-start(), calls=%async_computation.11 | async-start | bytes 7077888 | tf_op jit(solution)/shard_map/all_gather | solution.py:191
  97.5 730.0 %reduce-scatter.6.cloned.1.call-start = ((), (), s32[]{:S(2)}) async-start(), calls=%async_computation.12 | async-start | bytes 4456448 | tf_op jit(solution)/shard_map/reduce_scatter | solution.py:285
  97.6 57.5 %copy-start.41 = (f32[128]{0:T(128)S(1)}, f32[128]{0:T(128)}, u32[]{:S(2)}) copy-start(f32[128]{0:T(128)} %param.32) | copy-start | bytes 1540
  285.0 38.0 %copy-start.40 = (f32[1024]{0:T(1024)S(1)}, f32[1024]{0:T(1024)}, u32[]{:S(2)}) copy-start(f32[1024]{0:T(1024)} %param.31) | copy-start | bytes 12292
  286.7 110.2 %copy-start.24 = (bf16[8,2,128,128]{2,3,1,0:T(8,128)(2,1)}, bf16[8,2,128,128]{2,3,1,0:T(8,128)(2,1)S(1)}, u32[]{:S(2)}) copy-start(bf16[8,2,128,128]{2,3,1,0:T(8,128)(2,1)S(1)} %fusion.77) | copy-start | bytes 1572868
  323.0 228.9 %copy-start.14 = (f32[128,1024]{1,0:T(8,128)}, f32[128,1024]{1,0:T(8,128)S(1)}, u32[]{:S(2)}) copy-start(f32[128,1024]{1,0:T(8,128)S(1)} %get-tuple-element.620) | copy-start | bytes 1572868
  464.8 72.8 %copy-start.33 = (bf16[128,1024]{1,0:T(8,128)(2,1)S(1)}, bf16[128,1024]{1,0:T(8,128)(2,1)}, u32[]{:S(2)}) copy-start(bf16[128,1024]{1,0:T(8,128)(2,1)} %param.22) | copy-start | bytes 786436
  621.5 289.9 %reduce-scatter.10.cloned.1.call-start = ((), (), s32[]{:S(2)}) async-start(), calls=%async_computation.15 | async-start | bytes 4456448 | tf_op jit(solution)/shard_map/convert_element_type | solution.py:301
  635.3 612.2 %reduce-scatter.8.cloned.1.call-start = ((), (), s32[]{:S(2)}) async-start(), calls=%async_computation.13 | async-start | bytes 35389440 | tf_op jit(solution)/shard_map/reduce_scatter | solution.py:323
  640.6 188.2 %copy-start.13 = (f32[128,1024]{1,0:T(8,128)S(1)}, f32[128,1024]{1,0:T(8,128)}, u32[]{:S(2)}) copy-start(f32[128,1024]{1,0:T(8,128)} %copy-done.12) | copy-start | bytes 1572868
  937.3 310.3 %copy-start.15 = (f32[128,1024]{1,0:T(8,128)S(1)}, f32[128,1024]{1,0:T(8,128)}, u32[]{:S(2)}) copy-start(f32[128,1024]{1,0:T(8,128)} %copy-done.14) | copy-start | bytes 1572868
  937.3 460.7 %all-reduce.3.cloned.1.call-start = ((), (), s32[]{:S(2)}) async-start(), calls=%async_computation.14 | async-start | bytes 7864320 | tf_op jit(solution)/shard_map/psum | solution.py:340
  (32 other events, 132.3 us)
Sparse Core Ops, SparseCore 0:
  9.7 39.6 all-gather.9
  51.0 40.8 all-gather.15
  93.5 57.2 all-gather.13
  153.7 55.0 all-gather.11
  211.6 54.8 all-gather.17
  268.0 51.2 all-gather.19
  320.9 71.0 all-gather.21
  393.6 71.0 all-gather.23
  466.4 71.0 all-gather.25
  621.6 205.8 reduce-scatter.5
  832.1 79.1 reduce-scatter.9
  937.5 310.0 reduce-scatter.7
  1250.1 147.9 all-reduce.2
where the time goes:
time: 1420 us; the launch traced here: 1410 us
  waiting for transfers between devices  1120 us (79%)
  matrix products  90.4 us (6%)
  local copies, waits for them, and re-layouts  86.9 us (6%)
  blocking collectives  66.5 us (5%)
  other arithmetic  21.8 us (2%)
  between operations  14.8 us (1%)
    reduce_scatter x1, waiting for transfers between devices, on_device(): lax.psum_scatter(jnp.concatenate([rows_of(normed_in, d_query_b), rows_of(...  310 us
    reduce_scatter x1, waiting for transfers between devices, on_device(): lax.psum_scatter(key_acc.astype(jnp.bfloat16), 'ctx', scatter_dimension=0...  184 us
    convert_element_type x1, waiting for transfers between devices, on_device(): d_value.reshape(tok_rows, kv_heads * head_dim).astype(jnp.bfloat16)  77.6 us
    psum x1, waiting for transfers between devices, on_device(): lax.psum(shard_rows.astype(jnp.bfloat16), 'ctx').astype(jnp.float32)  73.1 us
    all_gather x1, waiting for transfers between devices, on_device(): lax.all_gather(w_gate, 'fsdp', axis=0, tiled=True)  68.8 us
    all_gather x1, waiting for transfers between devices, on_device(): lax.all_gather(w_up, 'fsdp', axis=0, tiled=True)  67.9 us
    all_gather x1, waiting for transfers between devices, on_device(): lax.all_gather(w_down, 'fsdp', axis=0, tiled=True)  67.8 us
    psum x1, blocking collectives, on_device(): lax.psum((norm_gain_part, mlp_gain_part, query_gain_part, key_gain_part),...  66.5 us
  transfers between devices with their start and end apart: 13, of which 13 were waited for; matrix products, arithmetic and copies ran while one was open for 6% of the time, Pallas kernels for 0%

commit v1 on v0

v1 whole, which is shorter than its diff:
```python
import math

import jax
import jax.numpy as jnp
import numpy as np
from jax import lax
from jax.experimental import pallas as pl
from jax.experimental.pallas import tpu as pltpu
from jax.sharding import PartitionSpec as P

MESH = pl.DeviceIdType.MESH
EPSILON = 1e-06
THETA = 1000000.0
HEAD_DIM = 128
SCALE = 1.0 / math.sqrt(HEAD_DIM)
SCALE_LOG2 = SCALE * math.log2(math.e)
F32 = jnp.float32
BF16 = jnp.bfloat16
DIST = (1, 3, 2)
SLOT = {1: 0, 3: 1, 2: 2}
COPIES = 256
COLS_MLP, COLS_OUT, COLS_QKV = 1152, 256, 512
FIRST = {COLS_MLP: 640, COLS_OUT: 128, COLS_QKV: 256}


def mm(left, right):
    return jnp.dot(left, right, preferred_element_type=F32)


def mm_last(left, right):
    return lax.dot_general(left, right, (((1,), (1,)), ((), ())), preferred_element_type=F32)


def mm_first(left, right):
    return lax.dot_general(left, right, (((0,), (0,)), ((), ())), preferred_element_type=F32)


def rms_scale(rows):
    return lax.rsqrt(jnp.mean(rows * rows, -1, keepdims=True) + EPSILON)


def swap_halves(heads):
    return pltpu.roll(heads, HEAD_DIM // 2, 1)


def rope_split(table):
    lane = lax.broadcasted_iota(jnp.int32, table.shape, 1)
    other = swap_halves(table)
    cosine = jnp.where(lane < HEAD_DIM // 2, table, other)
    sine = jnp.where(lane < HEAD_DIM // 2, -other, table)
    return cosine, sine


class Remote:
    def __init__(self, sems, src, dst, device, landing):
        send, recv, index = sems
        self.out = pltpu.make_async_remote_copy(
            src_ref=src,
            dst_ref=dst,
            send_sem=send.at[index],
            recv_sem=recv.at[index],
            device_id=device,
            device_id_type=MESH,
        )
        self.into = pltpu.make_async_remote_copy(
            src_ref=landing,
            dst_ref=landing,
            send_sem=send.at[index],
            recv_sem=recv.at[index],
            device_id=device,
            device_id_type=MESH,
        )

    def start(self):
        self.out.start()
        return self

    def wait_send(self):
        self.out.wait_send()

    def wait_recv(self):
        self.into.wait_recv()


def kernel(
    tok_ref, cot_ref, wq, wk, wv, wo, wg, wu, wd, ng_ref, mg_ref, qg_ref, kg_ref, rope_hbm,
    mixed_ref, ig_ref, out_m, out_o, out_a, gains_ref,
    g1, g2, g3, g4, w_a, w_o, w_m, raw, qh, kk, vx, rope, oa, att, do, dq, dk, dv, dqkv,
    hid, dgu, lse_row, delta_row, resid, d_resid,
    rs_send, rs_sib, rs_x, dkv_send, dkv_recv,
    gw_m, gw_o, gw_a, z1_m, z1_o, z1_a, y1_m, y1_o, y1_a,
    z2s_m, z2s_o, z2s_a, y2s_m, y2s_o, y2s_a, y2_m, y2_o, y2_a, z2_m, z2_o, z2_a,
    f_m, f_o, f_a, gain_own, gain_sib, gain_x, gain_y, gain_z,
    send, recv, local_sem,
):
    f_index = lax.axis_index("fsdp")
    c_index = lax.axis_index("ctx")
    z = lax.rem(f_index, 4)
    ylo = lax.div(f_index, 4)
    core = lax.rem(c_index, 2)
    x = lax.rem(lax.div(c_index, 2), 4)
    yhi = lax.div(c_index, 8)
    y = yhi * 2 + ylo
    slice_index = x * 2 + core

    def wrap(value):
        return lax.rem(value + 8, 4)

    def device(dx=0, dy=0, dz=0, dcore=0):
        to_x, to_y, to_z = wrap(x + dx), wrap(y + dy), wrap(z + dz)
        to_core = lax.rem(core + dcore, 2)
        return {
            "fsdp": lax.rem(to_y, 2) * 4 + to_z,
            "ctx": lax.div(to_y, 2) * 8 + to_x * 2 + to_core,
        }

    counter = [0]

    def sems():
        index = counter[0]
        counter[0] += 1
        assert index < COPIES
        return (send, recv, index)

    pending = []

    def remote(src, dst, to, landing):
        copy = Remote(sems(), src, dst, to, landing)
        copy.start()
        pending.append(copy)
        return copy

    def drain():
        while pending:
            pending.pop().wait_send()

    def rows(which):
        return pl.ds(pl.multiple_of(which * 128, 128), 128)

    mine, theirs = rows(core), rows(1 - core)
    sibling = device(dcore=1)
    partners = [sibling]
    partners += [device(dx=d) for d in DIST]
    partners += [device(dy=d) for d in DIST]
    partners += [device(dz=d) for d in DIST]
    partners += [device(dx=d, dy=2) for d in DIST]

    def columns(ref, width):
        return ref.at[:, pl.ds(pl.multiple_of(slice_index * width, 128), width)]

    local = []

    def fetch(src, dst):
        copy = pltpu.make_async_copy(src, dst, local_sem.at[len(local)])
        copy.start()
        local.append(copy)
        return copy

    fetch_a = [
        fetch(columns(wq, 256), w_a.at[f_index, :, 0:256]),
        fetch(columns(wk, 128), w_a.at[f_index, :, 256:384]),
        fetch(columns(wv, 128), w_a.at[f_index, :, 384:512]),
    ]
    fetch_o = [fetch(columns(wo, 256), w_o.at[f_index])]
    fetch_m = [
        fetch(columns(wg, 384), w_m.at[f_index, :, 0:384]),
        fetch(columns(wu, 384), w_m.at[f_index, :, 384:768]),
        fetch(columns(wd, 384), w_m.at[f_index, :, 768:1152]),
    ]
    fetch_rope = fetch(rope_hbm.at[pl.ds(yhi * 4, 4)], rope)

    barrier = pltpu.get_barrier_semaphore()
    for partner in partners:
        pl.semaphore_signal(barrier, inc=1, device_id=partner, device_id_type=MESH)

    class Gather:
        def __init__(self, ref):
            self.ref = ref
            own = ref.at[x, mine]
            self.ring = {
                d: remote(own, own, device(dx=d), ref.at[wrap(x - d), mine]) for d in DIST
            }
            self.pair = {0: remote(own, own, sibling, ref.at[x, theirs])}

        def forward(self, d):
            self.ring[d].wait_recv()
            block = self.ref.at[wrap(x - d), mine]
            self.pair[d] = remote(block, block, sibling, self.ref.at[wrap(x - d), theirs])

        def ready(self, d):
            self.pair[d].wait_recv()

    class Scatter:
        def __init__(self, index, buffer):
            self.part = rs_send.at[buffer]
            self.pair = rs_sib.at[index]
            self.ring = rs_x.at[index]
            self.pair_copy = {}
            self.ring_copy = {}

        def emit(self, d, value):
            self.part[d] = value.astype(BF16)
            self.pair_copy[d] = remote(
                self.part.at[d, theirs], self.pair.at[d], sibling, self.pair.at[d]
            )

        def forward(self, d):
            self.pair_copy[d].wait_recv()
            total = self.part[d, mine, :].astype(F32) + self.pair[d].astype(F32)
            self.pair[d] = total.astype(BF16)
            slot = self.ring.at[SLOT[d]]
            self.ring_copy[d] = remote(self.pair.at[d], slot, device(dx=d), slot)

        def release(self):
            for copy in self.pair_copy.values():
                copy.wait_send()
                pending.remove(copy)

        def total(self):
            self.pair_copy[0].wait_recv()
            value = self.part[0, mine, :].astype(F32) + self.pair[0].astype(F32)
            for d in DIST:
                self.ring_copy[d].wait_recv()
                value = value + self.ring[SLOT[d]].astype(F32)
            return value

    class WeightGather:
        def __init__(self, ref, fetched):
            self.ref = ref
            for copy in fetched:
                copy.wait()
            own = ref.at[f_index]
            self.along_z = {
                d: remote(own, own, device(dz=d), ref.at[ylo * 4 + wrap(z - d)]) for d in DIST
            }
            self.along_y = []
            self.spread(0)

        def spread(self, d):
            if d:
                self.along_z[d].wait_recv()
            held = ylo * 4 + wrap(z - d)
            coming = (1 - ylo) * 4 + wrap(z - d)
            for dy, part in ((1, pl.ds(0, 64)), (3, pl.ds(64, 64))):
                block = self.ref.at[held, part]
                self.along_y.append(
                    remote(block, block, device(dy=dy), self.ref.at[coming, part])
                )

        def finish(self):
            for copy in self.along_y:
                copy.wait_recv()

    class WeightGrad:
        def __init__(self, cols, gw, z1, y1, z2s, y2s, y2, z2, full, out):
            self.cols, self.gw, self.z1, self.y1 = cols, gw, z1, y1
            self.z2s, self.y2s, self.y2, self.z2 = z2s, y2s, y2, z2
            self.full, self.out = full, out
            self.left = slice(0, FIRST[cols])
            self.right = slice(FIRST[cols], cols)

        def stage_one(self):
            self.one_z, self.one_y = {}, {}
            for d in DIST:
                to_z, to_y = wrap(z + d), wrap(y + d)
                slot = self.z1.at[SLOT[d]]
                self.one_z[d] = remote(
                    self.gw.at[:, to_z, :, self.left], slot, device(dz=d), slot
                )
                slot = self.y1.at[SLOT[d]]
                half = pl.ds(pl.multiple_of(lax.div(to_y, 2) * 64, 64), 64)
                self.one_y[d] = remote(
                    self.gw.at[lax.rem(to_y, 2), :, half, self.right], slot, device(dy=d), slot
                )

        def stage_two(self):
            for d in DIST:
                self.one_z[d].wait_recv()
            total = self.gw[:, z, :, self.left].astype(F32)
            for d in DIST:
                total = total + self.z1[SLOT[d]].astype(F32)
            self.z2s[...] = total.astype(BF16).reshape(self.z2s.shape)
            self.two_y, self.two_z = {}, {}
            for d in DIST:
                to_y = wrap(y + d)
                slot = self.y2.at[SLOT[d]]
                self.two_y[d] = remote(
                    self.z2s.at[lax.rem(to_y, 2), lax.div(to_y, 2)], slot, device(dy=d), slot
                )
            for d in DIST:
                self.one_y[d].wait_recv()
            half = pl.ds(pl.multiple_of(yhi * 64, 64), 64)
            total = self.gw[ylo, :, half, self.right].astype(F32)
            for d in DIST:
                total = total + self.y1[SLOT[d]].astype(F32)
            self.y2s[...] = total.astype(BF16)
            for d in DIST:
                slot = self.z2.at[SLOT[d]]
                self.two_z[d] = remote(self.y2s.at[wrap(z + d)], slot, device(dz=d), slot)

        def stage_three(self):
            for d in DIST:
                self.two_y[d].wait_recv()
            total = self.z2s[ylo, yhi].astype(F32)
            for d in DIST:
                total = total + self.y2[SLOT[d]].astype(F32)
            self.full[yhi, x, core, :, self.left] = total.astype(BF16)
            for d in DIST:
                self.two_z[d].wait_recv()
            total = self.y2s[z].astype(F32)
            for d in DIST:
                total = total + self.z2[SLOT[d]].astype(F32)
            self.full[yhi, x, core, :, self.right] = total.astype(BF16)
            own = self.full.at[yhi, x, core]
            self.three = []
            for flip in (0, 1):
                for d in (0,) + DIST:
                    if d or flip:
                        from_hi = 1 - yhi if flip else yhi
                        self.three.append(
                            remote(
                                own, own, device(dx=d, dy=2 * flip),
                                self.full.at[from_hi, wrap(x - d), core],
                            )
                        )

        def stage_four(self):
            for copy in self.three:
                copy.wait_recv()
            held = self.full.at[:, :, core]
            self.four = remote(held, held, sibling, self.full.at[:, :, 1 - core])

        def stage_five(self):
            self.four.wait_recv()
            fetch(self.full, self.out)

    grad_m = WeightGrad(COLS_MLP, gw_m, z1_m, y1_m, z2s_m, y2s_m, y2_m, z2_m, f_m, out_m)
    grad_o = WeightGrad(COLS_OUT, gw_o, z1_o, y1_o, z2s_o, y2s_o, y2_o, z2_o, f_o, out_o)
    grad_a = WeightGrad(COLS_QKV, gw_a, z1_a, y1_a, z2s_a, y2s_a, y2_a, z2_a, f_a, out_a)

    def weight_grad(gw, parts):
        def chunk(index, carry):
            lanes = pl.ds(pl.multiple_of(index * 256, 256), 256)
            for left, right, cols in parts:
                value = mm_first(
                    left[:, :, lanes].reshape(1024, 256),
                    right[...].reshape(1024, right.shape[-1]),
                )
                block = pl.ds(lax.rem(index, 2) * 2, 2)
                gw[lax.div(index, 2), block, :, cols] = value.astype(BF16).reshape(
                    2, 128, right.shape[-1]
                )
            return carry

        lax.fori_loop(0, 4, chunk, 0)

    with jax.named_scope("first_norm"):
        inputs = tok_ref[...].astype(F32)
        g1[x, mine, :] = (inputs * rms_scale(inputs) * ng_ref[...]).astype(BF16)
        g3[x, mine, :] = cot_ref[...]
        vx[:, :, 128:256] = jnp.ones((8, 256, 128), BF16)
        gain_own[...] = jnp.zeros_like(gain_own)
    with jax.named_scope("entry_barrier"):
        pl.semaphore_wait(barrier, len(partners))
    with jax.named_scope("gather_start"):
        rows_one = Gather(g1)
        gather_a = WeightGather(w_a, fetch_a)
        for d in DIST:
            gather_a.spread(d)
            rows_one.forward(d)
        gather_o = WeightGather(w_o, fetch_o)
        gather_m = WeightGather(w_m, fetch_m)
        rows_cot = Gather(g3)
        gather_a.finish()
        fetch_rope.wait()

    def project(t):
        value = mm(g1[t], w_a[...].reshape(1024, COLS_QKV))
        cosine, sine = rope_split(rope[t])
        raw[t] = value[:, 0:384]
        for head in range(3):
            one = value[:, head * 128 : head * 128 + 128]
            gain = qg_ref[...] if head < 2 else kg_ref[...]
            scaled = one * rms_scale(one) * gain
            turned = (scaled * cosine + swap_halves(scaled) * sine).astype(BF16)
            if head < 2:
                qh[t, head * 256 : head * 256 + 256, :] = turned
            else:
                kk[yhi * 4 + t] = turned
        vx[yhi * 4 + t, :, 0:128] = value[:, 384:512].astype(BF16)

    with jax.named_scope("qkv"):
        for d in (0,) + DIST:
            rows_one.ready(d)
            project(wrap(x - d))

    across = device(dy=2)
    keys_half = kk.at[0:4]
    values_half = vx.at[0:4, :, 0:128]
    send_keys = Remote(sems(), keys_half, keys_half, across, keys_half)
    send_values = Remote(sems(), values_half, values_half, across, values_half)

    @pl.when(yhi == 0)
    def _():
        send_keys.start()
        send_values.start()

    def scores_full(i, key_rows):
        return jnp.exp2(mm_last(qh[i], key_rows) * SCALE_LOG2)

    def attend_own(i, carry):
        row = lax.broadcasted_iota(jnp.int32, (512, 256), 0)
        col = lax.broadcasted_iota(jnp.int32, (512, 256), 1)
        soft = jnp.where(col <= lax.rem(row, 256), scores_full(i, kk[yhi * 4 + i]), 0.0)
        oa[i] = mm(soft.astype(BF16), vx[yhi * 4 + i])

        def inner(j, carry):
            soft = scores_full(i, kk[yhi * 4 + j]).astype(BF16)
            oa[i] += mm(soft, vx[yhi * 4 + j])
            return carry

        lax.fori_loop(0, i, inner, 0)
        return carry

    with jax.named_scope("attend_own"):
        lax.fori_loop(0, 4, attend_own, 0)
    with jax.named_scope("spread_weights"):
        for d in DIST:
            gather_o.spread(d)
        for d in DIST:
            gather_m.spread(d)
        for d in DIST:
            rows_cot.forward(d)

    with jax.named_scope("attend_across"):

        @pl.when(yhi == 1)
        def _():
            send_keys.wait_recv()
            send_values.wait_recv()

            def attend_across(step, carry):
                i, j = lax.div(step, 2), lax.rem(step, 2)
                two = pl.ds(j * 2, 2)
                soft = scores_full(i, kk[two].reshape(512, 128)).astype(BF16)
                oa[i] += mm(soft, vx[two].reshape(512, 256))
                return carry

            lax.fori_loop(0, 8, attend_across, 0)

    with jax.named_scope("attend_end"):

        def attend_end(i, carry):
            both = oa[i]
            total = both[:, 128:256]
            exact = both[:, 0:128] / total
            oa[i, :, 0:128] = exact
            lse_row[i] = jnp.transpose(jnp.log(total) * math.log2(math.e))[0:8, :]
            att[i, :, 0:128] = exact[0:256].astype(BF16)
            att[i, :, 128:256] = exact[256:512].astype(BF16)
            return carry

        lax.fori_loop(0, 4, attend_end, 0)

    with jax.named_scope("branch"):
        gather_o.finish()
        branch = Scatter(0, 0)
        order = (2, 1, 3, 0)
        for place, d in enumerate(order):
            branch.emit(d, mm_last(att[wrap(x + d)], w_o[...].reshape(1024, COLS_OUT)))
            if place:
                branch.forward(order[place - 1])
    with jax.named_scope("resid"):
        value = branch.total() + tok_ref[...].astype(F32)
        resid[...] = value
        g2[x, mine, :] = (value * rms_scale(value) * mg_ref[...]).astype(BF16)
        rows_two = Gather(g2)
        gather_m.finish()
        branch.release()

    back_two = Scatter(1, 1)
    mlp_out = Scatter(2, 0)

    def feed_forward(d):
        t = wrap(x - d)
        w_gate_up = w_m[:, :, 0:768].reshape(1024, 768)
        w_d = w_m[:, :, 768:1152].reshape(1024, 384)
        both = mm(g2[t], w_gate_up)
        d_hidden = mm(g3[t], w_d)
        gate, up = both[:, 0:384], both[:, 384:768]
        sig = jax.nn.sigmoid(gate)
        active = gate * sig
        hid[t] = (active * up).astype(BF16)
        dgu[t, :, 0:384] = (d_hidden * up * sig * (1.0 + gate * (1.0 - sig))).astype(BF16)
        dgu[t, :, 384:768] = (d_hidden * active).astype(BF16)
        back_two.emit((4 - d) % 4, mm_last(dgu[t], w_gate_up))

    def feed_forward_out(d):
        w_d = w_m[:, :, 768:1152].reshape(1024, 384)
        mlp_out.emit((4 - d) % 4, mm_last(hid[wrap(x - d)], w_d))

    with jax.named_scope("mlp"):
        rows_cot.ready(0)
        rows_two.ready(0)
        feed_forward(0)
        for place, d in enumerate(DIST):
            rows_two.forward(d)
            rows_cot.ready(d)
            rows_two.ready(d)
            feed_forward(d)
            if place:
                back_two.forward((4 - DIST[place - 1]) % 4)
        back_two.forward(2)
    with jax.named_scope("mlp_out"):
        for place, d in enumerate((2, 1, 3, 0)):
            feed_forward_out(d)
            if place:
                mlp_out.forward((4 - (2, 1, 3)[place - 1]) % 4)
    with jax.named_scope("mlp_weight_grads"):
        weight_grad(gw_m, ((g2, dgu, slice(0, 768)), (g3, hid, slice(768, 1152))))
        grad_m.stage_one()
    with jax.named_scope("d_resid"):
        d_normed = back_two.total()
        value = resid[...]
        scaling = rms_scale(value)
        normed = value * scaling
        gain_own[0:1, :] = jnp.sum(d_normed * normed, 0, keepdims=True)
        d_normed = d_normed * mg_ref[...]
        value = scaling * (
            d_normed - normed * jnp.mean(d_normed * normed, -1, keepdims=True)
        ) + cot_ref[...].astype(F32)
        d_resid[...] = value
        g4[x, mine, :] = value.astype(BF16)
        rows_back = Gather(g4)
    with jax.named_scope("mixed"):
        mixed_ref[...] = (resid[...] + mlp_out.total()).astype(BF16)

    def back_out(t):
        value = mm(g4[t], w_o[...].reshape(1024, COLS_OUT)).astype(BF16)
        do[t, 0:256, :] = value[:, 0:128]
        do[t, 256:512, :] = value[:, 128:256]
        product = do[t].astype(F32) * oa[t, :, 0:128]
        delta_row[t] = jnp.broadcast_to(
            jnp.sum(jnp.transpose(product), 0, keepdims=True), (8, 512)
        )

    with jax.named_scope("d_attended"):
        rows_back.ready(0)
        back_out(x)
        for d in DIST:
            rows_back.forward(d)
            rows_back.ready(d)
            back_out(wrap(x - d))
    with jax.named_scope("out_weight_grads"):
        weight_grad(gw_o, ((g4, att, slice(0, 256)),))
        grad_o.stage_one()
        grad_m.stage_two()

    def tile(i, j, masked):
        key_rows, queries, grads = kk[j], qh[i], do[i]
        soft = jnp.exp2(mm_last(key_rows, queries) * SCALE_LOG2 - lse_row[i, 0:1, :])
        if masked:
            row = lax.broadcasted_iota(jnp.int32, (256, 512), 0)
            col = lax.broadcasted_iota(jnp.int32, (256, 512), 1)
            soft = jnp.where(row <= lax.rem(col, 256), soft, 0.0)
        d_soft = mm_last(vx[j, :, 0:128], grads)
        d_scores = (soft * (d_soft - delta_row[i, 0:1, :])).astype(BF16)
        dv[j] += mm(soft.astype(BF16), grads)
        dk[j] += mm(d_scores, queries)
        dq[i] += mm_first(d_scores, key_rows)

    with jax.named_scope("attend_back_across"):
        dq[...] = jnp.zeros_like(dq)
        dk[...] = jnp.zeros_like(dk)
        dv[...] = jnp.zeros_like(dv)

        send_back = Remote(sems(), dkv_send, dkv_recv, across, dkv_recv)

        @pl.when(yhi == 1)
        def _():
            def back_across(step, carry):
                tile(lax.rem(step, 4), lax.div(step, 4), False)
                return carry

            lax.fori_loop(0, 16, back_across, 0)
            dkv_send[0] = dk[0:4].astype(BF16)
            dkv_send[1] = dv[0:4].astype(BF16)
            send_back.start()

    with jax.named_scope("grad_stages"):
        grad_m.stage_three()
        grad_o.stage_two()

    with jax.named_scope("attend_back_own"):

        def back_own(i, carry):
            tile(i, yhi * 4 + i, True)

            def inner(j, carry):
                tile(i, yhi * 4 + j, False)
                return carry

            lax.fori_loop(0, i, inner, 0)
            return carry

        lax.fori_loop(0, 4, back_own, 0)

    with jax.named_scope("grad_stages_two"):
        grad_m.stage_four()
        grad_o.stage_three()

    with jax.named_scope("head_norm_back"):

        @pl.when(yhi == 0)
        def _():
            send_back.wait_recv()
            dk[0:4] += dkv_recv[0].astype(F32)
            dv[0:4] += dkv_recv[1].astype(F32)

        def head_back(t, carry):
            q_sum, k_sum = carry
            cosine, sine = rope_split(rope[t])
            for head in range(3):
                one = raw[t, :, head * 128 : head * 128 + 128]
                if head < 2:
                    grads, gain = dq[t, head * 256 : head * 256 + 256, :], qg_ref[...]
                else:
                    grads, gain = dk[yhi * 4 + t], kg_ref[...]
                grads = grads * SCALE
                grads = grads * cosine - swap_halves(grads) * sine
                scaling = rms_scale(one)
                normed = one * scaling
                part = jnp.sum(grads * normed, 0, keepdims=True)
                if head < 2:
                    q_sum = q_sum + part
                else:
                    k_sum = k_sum + part
                grads = grads * gain
                value = scaling * (grads - normed * jnp.mean(grads * normed, -1, keepdims=True))
                dqkv[t, :, head * 128 : head * 128 + 128] = value.astype(BF16)
            dqkv[t, :, 384:512] = dv[yhi * 4 + t].astype(BF16)
            return q_sum, k_sum

        zero = jnp.zeros((1, 128), F32)
        q_sum, k_sum = lax.fori_loop(0, 4, head_back, (zero, zero))
        gain_own[2:3, 0:128] = q_sum
        gain_own[2:3, 128:256] = k_sum

    with jax.named_scope("d_normed"):
        back_two.release()
        back_one = Scatter(3, 1)
        for place, d in enumerate(order):
            back_one.emit(d, mm_last(dqkv[wrap(x + d)], w_a[...].reshape(1024, COLS_QKV)))
            if place:
                back_one.forward(order[place - 1])
    with jax.named_scope("qkv_weight_grads"):
        weight_grad(gw_a, ((g1, dqkv, slice(0, 512)),))
        grad_a.stage_one()
        grad_m.stage_five()
        grad_o.stage_four()
    with jax.named_scope("input_grad"):
        d_normed = back_one.total()
        inputs = tok_ref[...].astype(F32)
        scaling = rms_scale(inputs)
        normed = inputs * scaling
        gain_own[1:2, :] = jnp.sum(d_normed * normed, 0, keepdims=True)
        d_normed = d_normed * ng_ref[...]
        ig_ref[...] = (
            scaling * (d_normed - normed * jnp.mean(d_normed * normed, -1, keepdims=True))
            + d_resid[...]
        )

    def ring_sum(slots, place, value, reach):
        slots[place] = value
        copies = []
        for d in DIST:
            own = slots.at[place]
            copies.append(remote(own, own, reach(d), slots.at[wrap(place - d)]))
        return copies

    def ring_total(slots, copies):
        for copy in copies:
            copy.wait_recv()
        return ((slots[0] + slots[1]) + slots[2]) + slots[3]

    with jax.named_scope("tail"):
        pair = remote(gain_own, gain_sib, sibling, gain_sib)
        pair.wait_recv()
        copies = ring_sum(gain_x, x, gain_own[...] + gain_sib[...], lambda d: device(dx=d))
        grad_a.stage_two()
        value = ring_total(gain_x, copies)
        copies = ring_sum(gain_y, y, value, lambda d: device(dy=d))
        grad_o.stage_five()
        grad_a.stage_three()
        value = ring_total(gain_y, copies)
        copies = ring_sum(gain_z, z, value, lambda d: device(dz=d))
        gains_ref[...] = ring_total(gain_z, copies)
        grad_a.stage_four()
        grad_a.stage_five()
    with jax.named_scope("drain"):
        drain()

        @pl.when(yhi == 0)
        def _():
            send_keys.wait_send()
            send_values.wait_send()

        @pl.when(yhi == 1)
        def _():
            send_back.wait_send()

        for copy in local[-3:]:
            copy.wait()


def rope_table(length):
    half = HEAD_DIM // 2
    freqs = np.power(np.float32(THETA), np.float32(-2.0) * np.arange(half, dtype=np.float32) / HEAD_DIM)
    angles = np.arange(length, dtype=np.float32)[:, None] * freqs.astype(np.float32)[None, :]
    table = np.concatenate([np.cos(angles), np.sin(angles)], 1).astype(np.float32)
    return table.reshape(length // 256, 256, HEAD_DIM)


def on_device(
    tokens, cotangent, w_query, w_key, w_value, w_output, w_gate, w_up, w_down,
    norm_gain, mlp_gain, query_gain, key_gain,
):
    vmem = pl.BlockSpec(memory_space=pltpu.VMEM)
    hbm = pl.BlockSpec(memory_space=pl.ANY)
    groups = (COLS_MLP, COLS_OUT, COLS_QKV)

    def v(shape, dtype=BF16):
        return pltpu.VMEM(shape, dtype)

    scratch = [v((4, 256, 1024)) for _ in range(4)]
    scratch += [v((8, 128, COLS_QKV)), v((8, 128, COLS_OUT)), v((8, 128, COLS_MLP))]
    scratch += [
        v((4, 256, 384), F32),
        v((4, 512, 128)),
        v((8, 256, 128)),
        v((8, 256, 256)),
        v((4, 256, 128), F32),
        v((4, 512, 256), F32),
        v((4, 256, 256)),
        v((4, 512, 128)),
        v((4, 512, 128), F32),
        v((8, 256, 128), F32),
        v((8, 256, 128), F32),
        v((4, 256, 512)),
        v((4, 256, 384)),
        v((4, 256, 768)),
        v((4, 8, 512), F32),
        v((4, 8, 512), F32),
        v((128, 1024), F32),
        v((128, 1024), F32),
        v((2, 4, 256, 1024)),
        v((4, 4, 128, 1024)),
        v((4, 3, 128, 1024)),
        v((2, 4, 256, 128)),
        v((2, 4, 256, 128)),
    ]
    scratch += [v((2, 4, 128, cols)) for cols in groups]
    scratch += [v((3, 2, 128, FIRST[cols])) for cols in groups]
    scratch += [v((3, 4, 64, cols - FIRST[cols])) for cols in groups]
    scratch += [v((2, 2, 64, FIRST[cols])) for cols in groups]
    scratch += [v((4, 64, cols - FIRST[cols])) for cols in groups]
    scratch += [v((3, 64, FIRST[cols])) for cols in groups]
    scratch += [v((3, 64, cols - FIRST[cols])) for cols in groups]
    scratch += [v((2, 4, 2, 64, cols)) for cols in groups]
    scratch += [v((8, 1024), F32), v((8, 1024), F32)]
    scratch += [v((4, 8, 1024), F32) for _ in range(3)]
    scratch += [
        pltpu.SemaphoreType.DMA((COPIES,)),
        pltpu.SemaphoreType.DMA((COPIES,)),
        pltpu.SemaphoreType.DMA((16,)),
    ]
    mixed, input_grad, full_m, full_o, full_a, gains = pl.pallas_call(
        kernel,
        name="layer",
        out_shape=(
            jax.ShapeDtypeStruct((128, 1024), BF16),
            jax.ShapeDtypeStruct((128, 1024), F32),
            *(jax.ShapeDtypeStruct((2, 4, 2, 64, cols), BF16) for cols in groups),
            jax.ShapeDtypeStruct((8, 1024), F32),
        ),
        in_specs=[vmem, vmem] + [hbm] * 7 + [vmem] * 4 + [hbm],
        out_specs=(vmem, vmem, hbm, hbm, hbm, vmem),
        scratch_shapes=scratch,
        compiler_params=pltpu.CompilerParams(
            collective_id=0, has_side_effects=True, vmem_limit_bytes=63 * 2**20
        ),
    )(
        tokens, cotangent, w_query, w_key, w_value, w_output, w_gate, w_up, w_down,
        norm_gain[None, :], mlp_gain[None, :], query_gain[None, :], key_gain[None, :],
        jnp.asarray(rope_table(2048)),
    )

    def whole(full, start, width):
        part = full[..., start : start + width].reshape(2, 8, 64, width)
        return part.transpose(0, 2, 1, 3).reshape(128, 8 * width).astype(F32)

    return (
        mixed,
        input_grad,
        whole(full_a, 0, 256),
        whole(full_a, 256, 128),
        whole(full_a, 384, 128),
        whole(full_o, 0, 256),
        whole(full_m, 0, 384),
        whole(full_m, 384, 384),
        whole(full_m, 768, 384),
        gains[1],
        gains[0],
        gains[2, 0:128],
        gains[2, 128:256],
    )


def solution(mesh):
    rows = P(("fsdp", "ctx"), None)
    weight = P("fsdp", None)
    return jax.shard_map(
        on_device,
        mesh=mesh,
        in_specs=(rows, rows) + (weight,) * 7 + (P(),) * 4,
        out_specs=(rows, rows) + (weight,) * 7 + (P(),) * 4,
        check_vma=False,
    )
```

time: 1420 us -> 222 us (0.16)
  waiting for transfers between devices: 1120 us -> 0 us
  Pallas kernels: 0 us -> 201 us
  matrix products: 90.4 us -> 0 us
  local copies, waits for them, and re-layouts: 86.9 us -> 18.9 us
  blocking collectives: 66.5 us -> 0 us
  other arithmetic: 21.8 us -> 0.76 us
    reduce_scatter x2 -> x0, waiting for transfers between devices: 493 us -> none  [the longest x1 310 us: on_device(): lax.psum_scatter(jnp.concatenate([rows_of(normed_in, d_query_b), rows_of(...]
    all_gather x9 -> x0, waiting for transfers between devices: 472 us -> none  [the longest x1 68.8 us: on_device(): lax.all_gather(w_gate, 'fsdp', axis=0, tiled=True)]
    pallas_call x0 -> x1, Pallas kernels: none -> 201 us  [on_device(): pl.pallas_call(kernel, name='layer', out_shape=(jax.ShapeDtypeStruct((128...]
    dot_general x28 -> x0, matrix products: 90.4 us -> none  [the longest x7 22.6 us: rows_of(): lax.dot_general(left, right, (((0,), (0,)), ((), ())), preferred_element_...]
    convert_element_type x1 -> x0, waiting for transfers between devices: 77.6 us -> none  [on_device(): d_value.reshape(tok_rows, kv_heads * head_dim).astype(jnp.bfloat16)]
    psum x1 -> x0, waiting for transfers between devices: 73.1 us -> none  [on_device(): lax.psum(shard_rows.astype(jnp.bfloat16), 'ctx').astype(jnp.float32)]
    psum x1 -> x0, blocking collectives: 66.5 us -> none  [on_device(): lax.psum((norm_gain_part, mlp_gain_part, query_gain_part, key_gain_part),...]
    dynamic_update_slice x2 -> x0, local copies, waits for them, and re-layouts: 22.5 us -> none  [the longest x1 11.2 us: gradient_update(): lax.dynamic_update_slice_in_dim(value_acc, lax.dynamic_slice_in_dim(value...]
  transfers between devices with their start and end apart: 13 -> 0, of which waited for: 13 -> 0; matrix products, arithmetic and copies ran while one was open for 6% -> 0% of each run, Pallas kernels for 0% -> 0%
where the time goes in v1:
time: 222 us; the launch traced here: 221 us
  Pallas kernels  201 us (91%)
  local copies, waits for them, and re-layouts  18.9 us (9%)
    pallas_call x1, Pallas kernels, on_device(): pl.pallas_call(kernel, name='layer', out_shape=(jax.ShapeDtypeStruct((128...  201 us
    unnamed x17, local copies, waits for them, and re-layouts  8.95 us
    convert_element_type x8, local copies, waits for them, and re-layouts, whole(): return part.transpose(0, 2, 1, 3).reshape(128, 8 * width).astype(F32)  5.75 us

profile of v1, /device:TPU:1, one launch (start us, length us, event | category | flops | bytes accessed | tf_op | source)
XLA Modules:
  0.0 221.4 jit_solution(14114565758613553734)
XLA Ops:
  0.6 201.0 %layer.1 = (bf16[128,1024]{1,0:T(8,128)(2,1)}, f32[128,1024]{1,0:T(8,128)}, bf16[2,4,2,64,1152]{4,3,2,1,0:T(8,128)(2,1)}, bf16[2,4,2,64,256]{4,3,2,1,0:T(8,128)(...) custom-call(bf16[128,1024]{1,0:T(8,128)(2,1)} %tok_ref.1, bf16[128,1024]{1,0:T(8,128)(2,1)} %cot_ref.1, ...), custom_call_target="tpu_custom_call" | custom-call | tf_op jit(solution)/shard_map/layer/pallas_call | solution.py:777
  201.6 1.1 fusion.1
  202.7 0.3 copy.28
  203.1 0.3 copy.29
  203.4 1.2 copy_bitcast_fusion
  204.6 0.6 copy-done
  205.2 0.4 fusion
  205.6 0.2 convert_bitcast_fusion.2
  205.8 0.9 copy.31
  206.7 1.4 copy.38
  208.1 0.2 convert_bitcast_fusion.1
  208.3 0.9 copy.32
  209.2 1.4 copy.39
  210.6 0.2 convert_bitcast_fusion
  210.8 0.9 copy.33
  211.7 1.4 copy.40
  213.1 1.4 fusion.2
  214.5 1.2 slice_bitcast_fusion
  215.9 0.6 copy.27
  216.5 1.3 copy.34
  218.0 0.6 copy.30
  218.6 1.3 copy.37
  219.9 0.7 copy.45
  220.6 0.8 copy.46
  (14 shorter events, 0.3 us)
Async XLA Ops:
  203.1 2.0 copy-start
  211.7 4.1 %copy-start.1 = (bf16[2,4,2,64,512]{4,3,2,1,0:T(8,128)(2,1)S(1)}, bf16[2,4,2,64,512]{4,3,2,1,0:T(8,128)(2,1)}, u32[]{:S(2)}) copy-start(bf16[2,4,2,64,512]{4,3,2,1,0:T(8,128)(2,1)} %get-tuple-element.21) | copy-start | bytes 3145732
  216.5 1.3 copy-start.2
  218.6 1.3 copy-start.4
  218.6 2.0 copy-start.3
